TPU v7x, 512 devices: a whole 4x8x8 slice. The times are simulated.
512 devices in a mesh: section: 4 (over y_lo, core), tensor: 8 (over z), ctx: 16 (over x, y_hi).
Axes of the slice: x: 4, y: 8 (y_hi: 4, y_lo: 2; y = y_hi * 2 + y_lo), z: 8, core: 2. Of those that a mesh axis runs over, the one named last changes fastest.
Arguments:
- gate_in: bfloat16 [4, 16384, 2048], P('section', 'ctx', 'tensor'), may hold values from -6 to 6
- value_in: bfloat16 [4, 16384, 2048], P('section', 'ctx', 'tensor'), may hold values from -6 to 6
- gate_out: bfloat16 [4, 16384, 2048], P('section', 'ctx', 'tensor'), may hold values from -6 to 6
- filter_spectrum: bfloat16 [4, 256, 2, 128, 2048], P('section', 'ctx', None, None, 'tensor'), may hold values from -16 to 16
- skip: bfloat16 [4, 2048], P('section', 'tensor'), may hold values from -4 to 4
- out_weight: bfloat16 [4, 2048, 4096], P('section', 'ctx', 'tensor'), may hold values from -0.125 to 0.125
Outputs:
- mixed: bfloat16 [4, 16384, 4096], P('section', 'ctx', 'tensor')
All inputs are finite; a program needn't handle non-finite values.
Results may differ from a plain program's by a relative error of at most 0.015.
Values may be sent and summed in bfloat16 or wider, within the bound.
A program may use at most 64 MiB of HBM per device.

v0:
```python
import math

import jax
import jax.numpy as jnp
from jax import lax
from jax.sharding import PartitionSpec as P

HIGHEST = lax.Precision.HIGHEST


def from_behind(value, axis, steps):
    count = lax.axis_size(axis)
    pairs = [(source, (source + steps) % count) for source in range(count)]
    return lax.ppermute(value, axis, pairs)


def phase_tables(first, second, modulus):
    turns = first[:, None] * second[None, :] % modulus
    phase = turns.astype(jnp.float32) * (2.0 * math.pi / modulus)
    return (jnp.cos(phase), jnp.sin(phase))


def rows_forward(values, col_start, row_count, col_count):
    half_rows = values.shape[0]
    freq_rows = jnp.arange(row_count, dtype=jnp.int32)
    cosine, sine_table = phase_tables(freq_rows, jnp.arange(half_rows, dtype=jnp.int32), row_count)
    real_part = jnp.einsum("kr,rsc->ksc", cosine, values, precision=HIGHEST)
    imag_part = -jnp.einsum("kr,rsc->ksc", sine_table, values, precision=HIGHEST)
    col_index = col_start + jnp.arange(values.shape[1], dtype=jnp.int32)
    twist_cos, twist_sin = phase_tables(freq_rows, col_index, row_count * col_count)
    twist_cos = twist_cos[:, :, None]
    twist_sin = twist_sin[:, :, None]
    new_real = real_part * twist_cos + imag_part * twist_sin
    new_imag = imag_part * twist_cos - real_part * twist_sin
    return jnp.stack([new_real, new_imag])


def cols_forward(stacked):
    index = jnp.arange(stacked.shape[2], dtype=jnp.int32)
    cosine, sine_table = phase_tables(index, index, stacked.shape[2])
    real_part = jnp.einsum("ms,ksc->kmc", cosine, stacked[0], precision=HIGHEST) + jnp.einsum(
        "ms,ksc->kmc", sine_table, stacked[1], precision=HIGHEST
    )
    imag_part = jnp.einsum("ms,ksc->kmc", cosine, stacked[1], precision=HIGHEST) - jnp.einsum(
        "ms,ksc->kmc", sine_table, stacked[0], precision=HIGHEST
    )
    return (real_part, imag_part)


def apply_filter(real_part, imag_part, response):
    resp_real = response[:, 0].astype(jnp.float32)
    resp_imag = response[:, 1].astype(jnp.float32)
    return (
        real_part * resp_real - imag_part * resp_imag,
        real_part * resp_imag + imag_part * resp_real,
    )


def cols_inverse(real_part, imag_part):
    index = jnp.arange(real_part.shape[1], dtype=jnp.int32)
    cosine, sine_table = phase_tables(index, index, real_part.shape[1])
    out_real = jnp.einsum("sm,kmc->ksc", cosine, real_part, precision=HIGHEST) - jnp.einsum(
        "sm,kmc->ksc", sine_table, imag_part, precision=HIGHEST
    )
    out_imag = jnp.einsum("sm,kmc->ksc", cosine, imag_part, precision=HIGHEST) + jnp.einsum(
        "sm,kmc->ksc", sine_table, real_part, precision=HIGHEST
    )
    return jnp.stack([out_real, out_imag])


def rows_inverse(stacked, col_start, half_rows, col_count):
    row_count = stacked.shape[1]
    freq_rows = jnp.arange(row_count, dtype=jnp.int32)
    col_index = col_start + jnp.arange(stacked.shape[2], dtype=jnp.int32)
    twist_cos, twist_sin = phase_tables(freq_rows, col_index, row_count * col_count)
    twist_cos = twist_cos[:, :, None]
    twist_sin = twist_sin[:, :, None]
    real_part = stacked[0] * twist_cos - stacked[1] * twist_sin
    imag_part = stacked[1] * twist_cos + stacked[0] * twist_sin
    cosine, sine_table = phase_tables(jnp.arange(half_rows, dtype=jnp.int32), freq_rows, row_count)
    result = jnp.einsum("rk,ksc->rsc", cosine, real_part, precision=HIGHEST) - jnp.einsum(
        "rk,ksc->rsc", sine_table, imag_part, precision=HIGHEST
    )
    return result * (1.0 / (row_count * col_count))


def to_rows(stacked):
    return lax.all_to_all(stacked, "ctx", split_axis=2, concat_axis=1, tiled=True)


def to_cols(stacked):
    return lax.all_to_all(stacked, "ctx", split_axis=1, concat_axis=2, tiled=True)


def per_device(gate_in, value_in, gate_out, filter_spectrum, skip, out_weight):
    products = (gate_in[0].astype(jnp.float32) * value_in[0].astype(jnp.float32)).astype(
        jnp.bfloat16
    )
    tok_count, chan_count = products.shape
    response = filter_spectrum[0]
    col_count = response.shape[2]
    ctx_size = lax.axis_size("ctx")
    row_count = 2 * tok_count * ctx_size // col_count
    col_start = lax.axis_index("ctx") * (col_count // ctx_size)
    values = products.astype(jnp.float32).reshape(1, tok_count // col_count, col_count, chan_count)
    values = to_rows(values)[0]
    stacked = to_cols(rows_forward(values, col_start, row_count, col_count))
    real_part, imag_part = cols_forward(stacked)
    real_part, imag_part = apply_filter(real_part, imag_part, response)
    stacked = to_rows(cols_inverse(real_part, imag_part))
    convolved = rows_inverse(stacked, col_start, row_count // 2, col_count)
    convolved = to_cols(convolved[None]).reshape(tok_count, chan_count)
    hidden = (
        (convolved + skip[0].astype(jnp.float32) * products.astype(jnp.float32))
        * gate_out[0].astype(jnp.float32)
    ).astype(jnp.bfloat16)
    features = lax.all_gather(hidden, "tensor", axis=1, tiled=True)
    weight_local = out_weight[0]
    layer_out = jnp.dot(
        features,
        lax.all_gather(weight_local, "ctx", axis=0, tiled=True),
        preferred_element_type=jnp.float32,
    ).astype(jnp.bfloat16)
    return from_behind(layer_out, "section", 1)[None]


def solution(mesh):
    placed = (
        P("section", "ctx", "tensor"),
        P("section", "ctx", "tensor"),
        P("section", "ctx", "tensor"),
        P("section", "ctx", None, None, "tensor"),
        P("section", "tensor"),
        P("section", "ctx", "tensor"),
    )
    return jax.shard_map(
        per_device,
        mesh=mesh,
        in_specs=placed,
        out_specs=P("section", "ctx", "tensor"),
        check_vma=False,
    )
```

profile of v0, /device:TPU:64, one launch (start us, length us, event | category | flops | bytes accessed | tf_op | source)
XLA Modules:
  0.0 455.3 jit_solution(317489938250434958)
XLA Ops:
  6.5 1.3 fusion.53
  7.9 1.6 copy.37
  9.4 9.7 %all-to-all-start = ((f32[1,8,128,256]{3,1,0,2:T(8,128)}), f32[1,8,128,256]{3,1,0,2:T(8,128)S(1)}, u32[]{:S(2)}, u32[]{:S(2)}) async-start(f32[1,8,128,256]{3,1,0,2:T(8,128)} %copy.37), calls=%async_computation | async-start | bytes 2097152 | tf_op jit(solution)/shard_map/all_to_all | solution.py:88
  19.1 0.1 fusion.111
  19.3 29.6 %all-to-all-done = f32[1,8,128,256]{3,1,0,2:T(8,128)S(1)} async-done(((f32[1,8,128,256]{3,1,0,2:T(8,128)}), f32[1,8,128,256]{3,1,0,2:T(8,128)S(1)}, u32[]{:S(2)}, u32[]{:S(2)}) %all-to-all-start) | async-done | bytes 1048608 | tf_op jit(solution)/shard_map/all_to_all | solution.py:88
  48.8 0.3 copy.92
  49.2 2.7 fusion.43
  51.8 3.2 add_bitcast_fusion.1
  55.1 0.4 pad_maximum_fusion
  55.5 4.4 copy.40
  59.9 4.5 all-to-all-start.1
  64.4 3.2 copy.46
  67.7 96.8 %all-to-all-done.1 = f32[2,256,8,256]{3,2,0,1:T(8,128)} async-done(((f32[2,256,8,256]{3,2,0,1:T(8,128)}), f32[2,256,8,256]{3,2,0,1:T(8,128)}, u32[]{:S(2)}, u32[]{:S(2)}) %all-to-all-start.1) | async-done | bytes 4194336 | tf_op jit(solution)/shard_map/all_to_all | solution.py:92
  164.5 2.5 copy.41
  167.0 0.4 fusion.165
  167.5 3.6 fusion.6
  171.1 3.6 fusion.4
  174.7 3.6 fusion.24
  178.4 4.1 fusion.27
  182.5 2.3 fusion.83
  184.7 2.3 fusion.81
  187.0 2.3 subtract_bitcast_fusion
  189.3 2.5 add_bitcast_fusion
  191.8 2.3 pad_maximum_fusion.1
  194.1 5.5 %copy.49 = f32[2,16,128,256]{3,1,0,2:T(8,128)} copy(f32[2,16,128,256]{2,3,1,0:T(8,128)} %pad_maximum_fusion.1) | data formatting | bytes 8388608 | tf_op jit(solution)/shard_map/stack | solution.py:68
  199.6 5.8 %all-to-all-start.2 = ((f32[2,16,128,256]{3,1,0,2:T(8,128)}), f32[2,16,128,256]{3,1,0,2:T(8,128)}, u32[]{:S(2)}, u32[]{:S(2)}) async-start(f32[2,16,128,256]{3,1,0,2:T(8,128)} %copy.49), calls=%async_computation.2 | async-start | bytes 8388608 | tf_op jit(solution)/shard_map/all_to_all | solution.py:88
  205.4 0.0 all-gather.6.cloned.1.call-start
  205.4 0.7 all-gather.6.cloned.1.call-update
  206.1 95.0 %all-to-all-done.2 = f32[2,16,128,256]{3,1,0,2:T(8,128)} async-done(((f32[2,16,128,256]{3,1,0,2:T(8,128)}), f32[2,16,128,256]{3,1,0,2:T(8,128)}, u32[]{:S(2)}, u32[]{:S(2)}) %all-to-all-start.2) | async-done | bytes 4194336 | tf_op jit(solution)/shard_map/all_to_all | solution.py:88
  301.1 4.6 %copy.91 = f32[2,16,128,256]{3,2,1,0:T(8,128)S(1)} copy(f32[2,16,128,256]{3,1,0,2:T(8,128)} %all-to-all-done.2) | data formatting | bytes 8388608 | tf_op jit(solution)/shard_map/all_to_all | solution.py:88
  305.7 0.4 fusion.164
  306.2 1.2 copy.51
  307.4 1.2 copy.52
  308.6 2.0 fusion.12
  310.6 2.0 fusion.39
  312.7 1.6 copy.53
  314.3 12.3 %all-to-all-start.3 = ((f32[1,128,8,256]{3,2,0,1:T(8,128)}), f32[1,128,8,256]{3,2,0,1:T(8,128)S(1)}, u32[]{:S(2)}, u32[]{:S(2)}) async-start(f32[1,128,8,256]{3,2,0,1:T(8,128)} %copy.53), calls=%async_computation.3 | async-start | bytes 2097152 | tf_op jit(solution)/shard_map/all_to_all | solution.py:92
  326.6 0.0 all-gather.4.cloned.1.call-start
  326.7 34.1 %all-to-all-done.3 = f32[1,128,8,256]{3,2,0,1:T(8,128)S(1)} async-done(((f32[1,128,8,256]{3,2,0,1:T(8,128)}), f32[1,128,8,256]{3,2,0,1:T(8,128)S(1)}, u32[]{:S(2)}, u32[]{:S(2)}) %all-to-all-start.3) | async-done | bytes 1048608 | tf_op jit(solution)/shard_map/all_to_all | solution.py:92
  360.8 0.1 copy.54
  360.9 1.1 fusion.42
  362.0 0.0 all-gather.4.cloned.1.call-update
  362.1 0.0 all-gather.6.cloned.1.call-done
  362.1 63.9 %all-gather.4.cloned.1.call-done = bf16[1024,2048]{1,0:T(8,128)(2,1)} async-done(((bf16[1024,256]{1,0:T(8,128)(2,1)}), bf16[1024,2048]{1,0:T(8,128)(2,1)}) %all-gather.4.cloned.1.call-update) | async-done | bytes 4194320 | tf_op jit(solution)/shard_map/all_gather | solution.py:117
  426.0 5.2 %fusion.30 = bf16[1024,512]{1,0:T(8,128)(2,1)S(1)} fusion(bf16[1024,2048]{1,0:T(8,128)(2,1)} %all-gather.4.cloned.1.call-done, bf16[1,2048,512]{2,1,0:T(8,128)(2,1)} %all-gather.6.cloned.1.call-done), kind=kOutput, calls=%fused_computation.37 | convolution fusion | flops 2148007936 | bytes 7340032 | tf_op jit(solution)/shard_map/dot_general | solution.py:119
  431.2 1.9 collective-permute-start
  433.1 14.2 %collective-permute-done = bf16[1024,512]{1,0:T(8,128)(2,1)S(1)} collective-permute-done((bf16[1024,512]{1,0:T(8,128)(2,1)S(1)}, bf16[1024,512]{1,0:T(8,128)(2,1)S(1)}, u32[]{:S(2)}, u32[]{:S(2)}) %collective-permute-start) | collective-permute-done | bytes 1048608 | tf_op jit(solution)/shard_map/ppermute | solution.py:14
  447.3 1.0 copy.94
  (10 shorter events, 0.0 us)
Async XLA Ops:
  9.4 39.4 %all-to-all-start = ((f32[1,8,128,256]{3,1,0,2:T(8,128)}), f32[1,8,128,256]{3,1,0,2:T(8,128)S(1)}, u32[]{:S(2)}, u32[]{:S(2)}) async-start(f32[1,8,128,256]{3,1,0,2:T(8,128)} %copy.37), calls=%async_computation | async-start | bytes 2097152 | tf_op jit(solution)/shard_map/all_to_all | solution.py:88
  59.9 104.6 %all-to-all-start.1 = ((f32[2,256,8,256]{3,2,0,1:T(8,128)}), f32[2,256,8,256]{3,2,0,1:T(8,128)}, u32[]{:S(2)}, u32[]{:S(2)}) async-start(f32[2,256,8,256]{3,2,0,1:T(8,128)} %copy.40), calls=%async_computation.1 | async-start | bytes 8388608 | tf_op jit(solution)/shard_map/all_to_all | solution.py:92
  199.6 101.5 %all-to-all-start.2 = ((f32[2,16,128,256]{3,1,0,2:T(8,128)}), f32[2,16,128,256]{3,1,0,2:T(8,128)}, u32[]{:S(2)}, u32[]{:S(2)}) async-start(f32[2,16,128,256]{3,1,0,2:T(8,128)} %copy.49), calls=%async_computation.2 | async-start | bytes 8388608 | tf_op jit(solution)/shard_map/all_to_all | solution.py:88
  205.4 156.7 %all-gather.6.cloned.1.call-start = ((), (), s32[]{:S(2)}) async-start(), calls=%async_computation.5 | async-start | bytes 2228224 | tf_op jit(solution)/shard_map/all_gather | solution.py:121
  312.7 14.0 %copy-start.3 = (bf16[1,256]{1,0:T(2,128)(2,1)S(1)}, bf16[1,256]{1,0:T(2,128)(2,1)}, u32[]{:S(2)}) copy-start(bf16[1,256]{1,0:T(2,128)(2,1)} %param.10) | copy-start | bytes 1540
  314.3 46.6 %copy-start = (bf16[1,1024,256]{2,1,0:T(8,128)(2,1)S(1)}, bf16[1,1024,256]{2,1,0:T(8,128)(2,1)}, u32[]{:S(2)}) copy-start(bf16[1,1024,256]{2,1,0:T(8,128)(2,1)} %param.7) | copy-start | bytes 1572868
  314.3 46.6 %copy-start.1 = (bf16[1,1024,256]{2,1,0:T(8,128)(2,1)S(1)}, bf16[1,1024,256]{2,1,0:T(8,128)(2,1)}, u32[]{:S(2)}) copy-start(bf16[1,1024,256]{2,1,0:T(8,128)(2,1)} %param.6) | copy-start | bytes 1572868
  314.3 46.6 %copy-start.2 = (bf16[1,1024,256]{2,1,0:T(8,128)(2,1)S(1)}, bf16[1,1024,256]{2,1,0:T(8,128)(2,1)}, u32[]{:S(2)}) copy-start(bf16[1,1024,256]{2,1,0:T(8,128)(2,1)} %param.8) | copy-start | bytes 1572868
  314.3 46.5 %all-to-all-start.3 = ((f32[1,128,8,256]{3,2,0,1:T(8,128)}), f32[1,128,8,256]{3,2,0,1:T(8,128)S(1)}, u32[]{:S(2)}, u32[]{:S(2)}) async-start(f32[1,128,8,256]{3,2,0,1:T(8,128)} %copy.53), calls=%async_computation.3 | async-start | bytes 2097152 | tf_op jit(solution)/shard_map/all_to_all | solution.py:92
  326.6 99.4 %all-gather.4.cloned.1.call-start = ((), (), s32[]{:S(2)}) async-start(), calls=%async_computation.4 | async-start | bytes 4718592 | tf_op jit(solution)/shard_map/all_gather | solution.py:117
  431.2 16.1 %collective-permute-start = (bf16[1024,512]{1,0:T(8,128)(2,1)S(1)}, bf16[1024,512]{1,0:T(8,128)(2,1)S(1)}, u32[]{:S(2)}, u32[]{:S(2)}) collective-permute-start(bf16[1024,512]{1,0:T(8,128)(2,1)S(1)} %fusion.30), channel_id=1, source_target_pairs={{0,128},{128,256},{256,384},{384,0},{1,129},{129,257},{257,385},{3... | collective-permute-start | bytes 3145736 | tf_op jit(solution)/shard_map/ppermute | solution.py:14
Sparse Core Ops, SparseCore 0:
  209.2 138.1 all-gather.5
  362.2 63.7 all-gather.3
where the time goes:
time: 464 us; the launch traced here: 455 us
  waiting for transfers between devices  334 us (72%)
  matrix products  39.4 us (8%)
  starting transfers between devices  34.3 us (7%)
  local copies, waits for them, and re-layouts  28.2 us (6%)
  between operations  13.9 us (3%)
  other arithmetic  5.2 us (1%)
    all_to_all x2, waiting for transfers between devices, to_cols(): lax.all_to_all(stacked, 'ctx', split_axis=1, concat_axis=2, tiled=True)  131 us
    all_to_all x2, waiting for transfers between devices, to_rows(): lax.all_to_all(stacked, 'ctx', split_axis=2, concat_axis=1, tiled=True)  125 us
    all_gather x1, waiting for transfers between devices, per_device(): features = lax.all_gather(hidden, 'tensor', axis=1, tiled=True)  63.9 us
    all_to_all x2, starting transfers between devices, to_cols(): lax.all_to_all(stacked, 'ctx', split_axis=1, concat_axis=2, tiled=True)  16.8 us
    all_to_all x2, starting transfers between devices, to_rows(): lax.all_to_all(stacked, 'ctx', split_axis=2, concat_axis=1, tiled=True)  15.4 us
    ppermute x1, waiting for transfers between devices, from_behind(): return lax.ppermute(value, axis, pairs)  14.2 us
  transfers between devices with their start and end apart: 7, of which 6 were waited for; matrix products, arithmetic and copies ran while one was open for 4% of the time, Pallas kernels for 0%

commit v1 on v0

v1 whole, which is shorter than its diff:
```python
import functools
import math

import jax
import jax.numpy as jnp
import numpy as np
from jax import lax
from jax.experimental import pallas as pl
from jax.experimental.pallas import tpu as pltpu
from jax.sharding import PartitionSpec as P


def tables(rows, cols):
    total = rows * cols
    half = rows // 2
    k1 = np.arange(rows)
    angle = 2.0 * math.pi / rows * ((k1[:, None] * np.arange(half)[None, :]) % rows)
    first = np.concatenate([np.cos(angle), -np.sin(angle)], axis=0)
    s = np.arange(cols)
    angle = 2.0 * math.pi / cols * ((s[:, None] * s[None, :]) % cols)
    c, d = np.cos(angle), np.sin(angle)
    second = np.block([[c, -d], [d, c]])
    third = np.block([[c, d], [-d, c]])
    angle = 2.0 * math.pi / rows * ((np.arange(half)[:, None] * k1[None, :]) % rows)
    fourth = np.concatenate([np.cos(angle), -np.sin(angle)], axis=1) / total
    angle = 2.0 * math.pi / total * ((k1[:, None] * s[None, :]) % total)
    twist = np.stack([np.cos(angle), np.sin(angle)])
    cast = lambda m: jnp.asarray(m.astype(np.float32)).astype(jnp.bfloat16)
    return cast(first), cast(second), cast(third), cast(fourth), jnp.asarray(twist.astype(np.float32))


def conv_kernel(group, x_ref, f_ref, m1, m2, m3, m4, twist, o_ref):
    rows, cols = twist.shape[1:]
    dot = functools.partial(jnp.dot, preferred_element_type=jnp.float32)
    for c in range(group):
        tc, ts = twist[0], twist[1]
        y = dot(m1[...], x_ref[c])
        yr, yi = y[:rows], y[rows:]
        y = jnp.concatenate([yr * tc + yi * ts, yi * tc - yr * ts], axis=1)
        x = dot(y.astype(jnp.bfloat16), m2[...])
        xr, xi = x[:, :cols], x[:, cols:]
        hr = f_ref[c, :, :cols].astype(jnp.float32)
        hi = f_ref[c, :, cols:].astype(jnp.float32)
        z = jnp.concatenate([xr * hr - xi * hi, xr * hi + xi * hr], axis=1)
        v = dot(z.astype(jnp.bfloat16), m3[...])
        vr, vi = v[:, :cols], v[:, cols:]
        v = jnp.concatenate([vr * tc - vi * ts, vi * tc + vr * ts], axis=0)
        o_ref[c] = dot(m4[...], v.astype(jnp.bfloat16)).astype(o_ref.dtype)


def convolve(x, spectrum, group=2):
    chans, half, cols = x.shape
    rows = 2 * half
    consts = tables(rows, cols)
    whole = [pl.BlockSpec(c.shape, functools.partial(lambda n, i: (0,) * n, c.ndim)) for c in consts]
    return pl.pallas_call(
        functools.partial(conv_kernel, group),
        grid=(chans // group,),
        in_specs=[
            pl.BlockSpec((group, half, cols), lambda i: (i, 0, 0)),
            pl.BlockSpec((group, rows, 2 * cols), lambda i: (i, 0, 0)),
            *whole,
        ],
        out_specs=pl.BlockSpec((group, half, cols), lambda i: (i, 0, 0)),
        out_shape=jax.ShapeDtypeStruct(x.shape, jnp.bfloat16),
        cost_estimate=pl.CostEstimate(flops=2 * 800_000_000, bytes_accessed=6_000_000, transcendentals=0),
        compiler_params=pltpu.CompilerParams(vmem_limit_bytes=32 * 1024 * 1024),
    )(x, spectrum, *consts)


def per_device(gate_in, value_in, gate_out, filter_spectrum, skip, out_weight):
    products = (gate_in[0].astype(jnp.float32) * value_in[0].astype(jnp.float32)).astype(jnp.bfloat16)
    tok_count, chan_count = products.shape
    my_rows, _, cols, _ = filter_spectrum.shape[1:]
    spectrum = filter_spectrum[0].transpose(3, 0, 1, 2)
    spectrum = lax.all_to_all(spectrum, "ctx", split_axis=0, concat_axis=1, tiled=True)
    spectrum = spectrum.reshape(*spectrum.shape[:2], 2 * cols)
    x = products.reshape(tok_count // cols, cols, chan_count).transpose(2, 0, 1)
    x = lax.all_to_all(x, "ctx", split_axis=0, concat_axis=1, tiled=True)
    out = convolve(x, spectrum)
    out = lax.all_to_all(out, "ctx", split_axis=1, concat_axis=0, tiled=True)
    convolved = out.transpose(1, 2, 0).reshape(tok_count, chan_count).astype(jnp.float32)
    hidden = (
        (convolved + skip[0].astype(jnp.float32) * products.astype(jnp.float32))
        * gate_out[0].astype(jnp.float32)
    ).astype(jnp.bfloat16)
    count = lax.axis_size("section")
    pairs = [(source, (source + 1) % count) for source in range(count)]
    hidden = lax.ppermute(hidden, "section", pairs)
    weight = lax.ppermute(out_weight[0], "section", pairs)
    weight = lax.all_gather(weight, "ctx", axis=0, tiled=True)
    features = lax.all_gather(hidden, "tensor", axis=1, tiled=True)
    return jnp.dot(features, weight, preferred_element_type=jnp.float32).astype(jnp.bfloat16)[None]


def solution(mesh):
    placed = (
        P("section", "ctx", "tensor"),
        P("section", "ctx", "tensor"),
        P("section", "ctx", "tensor"),
        P("section", "ctx", None, None, "tensor"),
        P("section", "tensor"),
        P("section", "ctx", "tensor"),
    )
    return jax.shard_map(
        per_device,
        mesh=mesh,
        in_specs=placed,
        out_specs=P("section", "ctx", "tensor"),
        check_vma=False,
    )
```

time: 464 us -> 246 us (0.53)
  the two profiles are of different devices: /device:TPU:64 before, /device:TPU:1 now
where the time goes in v1:
time: 246 us; the launch traced here: 243 us
  waiting for transfers between devices  172 us (70%)
  starting transfers between devices  25.9 us (11%)
  local copies, waits for them, and re-layouts  14.8 us (6%)
  between operations  13.6 us (6%)
  Pallas kernels  8.38 us (3%)
  matrix products  6.16 us (3%)
    all_gather x1, waiting for transfers between devices, per_device(): features = lax.all_gather(hidden, 'tensor', axis=1, tiled=True)  65.1 us
    ppermute x1, waiting for transfers between devices, per_device(): weight = lax.ppermute(out_weight[0], 'section', pairs)  48.1 us
    all_to_all x1, waiting for transfers between devices, per_device(): out = lax.all_to_all(out, 'ctx', split_axis=1, concat_axis=0, tiled=True)  18.2 us
    ppermute x1, waiting for transfers between devices, per_device(): hidden = lax.ppermute(hidden, 'section', pairs)  14.9 us
    all_to_all x1, waiting for transfers between devices, per_device(): x = lax.all_to_all(x, 'ctx', split_axis=0, concat_axis=1, tiled=True)  14.1 us
    all_gather x1, waiting for transfers between devices, per_device(): weight = lax.all_gather(weight, 'ctx', axis=0, tiled=True)  10.5 us
    all_to_all x1, starting transfers between devices, per_device(): x = lax.all_to_all(x, 'ctx', split_axis=0, concat_axis=1, tiled=True)  10.2 us
    pallas_call x1, Pallas kernels, convolve(): pl.pallas_call(functools.partial(conv_kernel, group), grid=(chans // grou...  8.38 us
  transfers between devices with their start and end apart: 7, of which 7 were waited for; matrix products, arithmetic and copies ran while one was open for 5% of the time, Pallas kernels for 3%

profile of v1, /device:TPU:1, one launch (start us, length us, event | category | flops | bytes accessed | tf_op | source)
XLA Modules:
  0.0 242.8 jit_solution(9630544164774558923)
XLA Ops:
  6.5 0.0 copy-start.7
  6.5 1.5 multiply_convert_fusion
  8.0 0.0 copy-start.5
  8.0 1.1 copy.33
  9.1 10.2 %all-to-all-start = ((bf16[256,8,128]{2,1,0:T(8,128)(2,1)}), bf16[256,8,128]{2,1,0:T(8,128)(2,1)S(1)}, u32[]{:S(2)}, u32[]{:S(2)}) async-start(bf16[256,8,128]{2,1,0:T(8,128)(2,1)} %bitcast.41), calls=%async_computation | async-start | bytes 1048576 | tf_op jit(solution)/shard_map/all_to_all | solution.py:79
  19.3 0.0 copy-done.7
  19.3 3.1 %copy.27 = bf16[1,16,2,128,256]{3,1,2,4,0:T(8,128)(2,1)} copy(bf16[1,16,2,128,256]{4,3,2,1,0:T(8,128)(2,1)S(1)} %copy-done.7) | data formatting | bytes 4194304 | tf_op args[3]
  22.5 0.0 copy-done.5
  22.5 14.1 %all-to-all-done = bf16[256,8,128]{2,1,0:T(8,128)(2,1)S(1)} async-done(((bf16[256,8,128]{2,1,0:T(8,128)(2,1)}), bf16[256,8,128]{2,1,0:T(8,128)(2,1)S(1)}, u32[]{:S(2)}, u32[]{:S(2)}) %all-to-all-start) | async-done | bytes 524320 | tf_op jit(solution)/shard_map/all_to_all | solution.py:79
  36.6 4.7 %all-to-all-start.1 = ((bf16[256,16,2,128]{3,1,2,0:T(8,128)(2,1)}), bf16[256,16,2,128]{3,1,2,0:T(8,128)(2,1)S(1)}, u32[]{:S(2)}, u32[]{:S(2)}) async-start(bf16[256,16,2,128]{3,1,2,0:T(8,128)(2,1)} %bitcast.6), calls=%async_computation.1 | async-start | bytes 4194304 | tf_op jit(solution)/shard_map/all_to_all | solution.py:76
  41.3 0.0 all-gather.5.cloned.1.call-start
  41.3 0.0 copy-done.12
  41.3 2.8 %collective-permute-start.1 = (bf16[128,512]{1,0:T(8,128)(2,1)S(1)}, bf16[128,512]{1,0:T(8,128)(2,1)S(1)}, u32[]{:S(2)}, u32[]{:S(2)}) collective-permute-start(bf16[128,512]{1,0:T(8,128)(2,1)S(1)} %bitcast.43), channel_id=1, source_target_pairs={{0,128},{128,256},{256,384},{384,0},{1,129},{129,257},{257,385},{3... | collective-permute-start | bytes 393224 | tf_op jit(solution)/shard_map/ppermute | solution.py:90
  44.1 48.1 %collective-permute-done.1 = bf16[128,512]{1,0:T(8,128)(2,1)S(1)} collective-permute-done((bf16[128,512]{1,0:T(8,128)(2,1)S(1)}, bf16[128,512]{1,0:T(8,128)(2,1)S(1)}, u32[]{:S(2)}, u32[]{:S(2)}) %collective-permute-start.1) | collective-permute-done | bytes 131104 | tf_op jit(solution)/shard_map/ppermute | solution.py:90
  92.3 0.7 copy-done.10
  92.9 0.0 all-gather.5.cloned.1.call-update
  92.9 0.1 copy.37
  93.1 1.2 all-to-all-done.1
  94.2 3.5 %copy.28 = bf16[16,16,16,2,128]{4,3,2,1,0:T(2,128)(2,1)} copy(bf16[16,16,16,2,128]{4,2,3,0,1:T(8,128)(2,1)S(1)} %bitcast.37) | data formatting | bytes 4194304 | tf_op jit(solution)/shard_map/all_to_all | solution.py:76
  97.7 0.0 copy-start.4
  97.8 3.2 %reshape.24.f_ref = bf16[16,256,256]{2,1,0:T(8,128)(2,1)S(1)} reshape(bf16[16,16,16,2,128]{4,3,2,1,0:T(2,128)(2,1)} %copy.28) | data formatting | bytes 4194304 | tf_op jit(solution)/shard_map/reshape | solution.py:77
  101.0 0.0 copy-done
  101.0 0.0 copy-done.1
  101.0 0.0 copy-done.2
  101.0 0.0 copy-done.3
  101.0 0.0 copy-done.4
  101.0 8.4 %shard_map.109 = bf16[16,128,128]{2,1,0:T(8,128)(2,1)S(1)} custom-call(bf16[16,128,128]{2,1,0:T(8,128)(2,1)S(1)} %bitcast.36, bf16[16,256,256]{2,1,0:T(8,128)(2,1)S(1)} %reshape.24.f_ref, bf16[512,128]{1,0:T(8,128)(2,1)S(1)} %copy-done.1, bf16[256,256]{1,0:T(8,128)(2,1)S(1)} %copy-done.2, bf16[256,256]{1,0:T(8,128)(2,1)S(1)} %copy-done.3, ...), custom_call_target="tpu_custom_call" | custom-call | flops 1600000000 | bytes 6000000 | tf_op jit(solution)/shard_map/pallas_call | solution.py:56
  109.4 0.0 copy-start.11
  109.4 1.1 copy.29
  110.6 6.2 %all-to-all-start.2 = ((bf16[16,128,128]{2,0,1:T(8,128)(2,1)}), bf16[16,128,128]{2,0,1:T(8,128)(2,1)S(1)}, u32[]{:S(2)}, u32[]{:S(2)}) async-start(bf16[16,128,128]{2,0,1:T(8,128)(2,1)} %copy.29), calls=%async_computation.2 | async-start | bytes 1048576 | tf_op jit(solution)/shard_map/all_to_all | solution.py:81
  116.7 0.0 all-gather.3.cloned.1.call-start
  116.8 0.0 copy-done.11
  116.8 18.2 %all-to-all-done.2 = bf16[16,128,128]{2,0,1:T(8,128)(2,1)S(1)} async-done(((bf16[16,128,128]{2,0,1:T(8,128)(2,1)}), bf16[16,128,128]{2,0,1:T(8,128)(2,1)S(1)}, u32[]{:S(2)}, u32[]{:S(2)}) %all-to-all-start.2) | async-done | bytes 524320 | tf_op jit(solution)/shard_map/all_to_all | solution.py:81
  135.0 0.1 convert_bitcast_fusion
  135.1 0.0 copy-start.6
  135.1 0.0 copy-start.8
  135.1 0.1 copy.31
  135.2 0.4 copy.34
  135.6 0.5 copy-done.6
  136.1 0.2 copy-done.8
  136.3 0.2 fusion.1
  136.5 1.9 collective-permute-start
  138.4 14.9 %collective-permute-done = bf16[1024,256]{1,0:T(8,128)(2,1)S(1)} collective-permute-done((bf16[1024,256]{1,0:T(8,128)(2,1)S(1)}, bf16[1024,256]{1,0:T(8,128)(2,1)S(1)}, u32[]{:S(2)}, u32[]{:S(2)}) %collective-permute-start) | collective-permute-done | bytes 524320 | tf_op jit(solution)/shard_map/ppermute | solution.py:89
  153.3 0.8 copy-done.9
  154.1 0.0 all-gather.3.cloned.1.call-update
  154.2 10.5 %all-gather.5.cloned.1.call-done = bf16[2048,512]{1,0:T(8,128)(2,1)} async-done(((bf16[128,512]{1,0:T(8,128)(2,1)}), bf16[2048,512]{1,0:T(8,128)(2,1)}) %all-gather.5.cloned.1.call-update) | async-done | bytes 2097168 | tf_op jit(solution)/shard_map/all_gather | solution.py:91
  164.7 65.1 %all-gather.3.cloned.1.call-done = bf16[1024,2048]{1,0:T(8,128)(2,1)} async-done(((bf16[1024,256]{1,0:T(8,128)(2,1)}), bf16[1024,2048]{1,0:T(8,128)(2,1)}) %all-gather.3.cloned.1.call-update) | async-done | bytes 4194320 | tf_op jit(solution)/shard_map/all_gather | solution.py:92
  229.8 6.2 %fusion = bf16[1,1024,512]{2,1,0:T(8,128)(2,1)} fusion(bf16[1024,2048]{1,0:T(8,128)(2,1)} %all-gather.3.cloned.1.call-done, bf16[2048,512]{1,0:T(8,128)(2,1)} %all-gather.5.cloned.1.call-done), kind=kOutput, calls=%fused_computation.1 | convolution fusion | flops 2148007936 | bytes 7340032 | tf_op jit(solution)/shard_map/dot_general | solution.py:93
  (8 shorter events, 0.0 us)
Async XLA Ops:
  6.5 12.8 %copy-start.7 = (bf16[1,16,2,128,256]{4,3,2,1,0:T(8,128)(2,1)S(1)}, bf16[1,16,2,128,256]{4,3,2,1,0:T(8,128)(2,1)}, u32[]{:S(2)}) copy-start(bf16[1,16,2,128,256]{4,3,2,1,0:T(8,128)(2,1)} %param.14) | copy-start | bytes 6291460
  8.0 14.4 %copy-start.5 = (bf16[1,1024,256]{2,1,0:T(8,128)(2,1)}, bf16[1,1024,256]{2,1,0:T(8,128)(2,1)S(1)}, u32[]{:S(2)}) copy-start(bf16[1,1024,256]{2,1,0:T(8,128)(2,1)S(1)} %multiply_convert_fusion) | copy-start | bytes 1572868
  9.1 27.5 %all-to-all-start = ((bf16[256,8,128]{2,1,0:T(8,128)(2,1)}), bf16[256,8,128]{2,1,0:T(8,128)(2,1)S(1)}, u32[]{:S(2)}, u32[]{:S(2)}) async-start(bf16[256,8,128]{2,1,0:T(8,128)(2,1)} %bitcast.41), calls=%async_computation | async-start | bytes 1048576 | tf_op jit(solution)/shard_map/all_to_all | solution.py:79
  36.6 4.8 %copy-start.12 = (bf16[1,128,512]{2,1,0:T(8,128)(2,1)S(1)}, bf16[1,128,512]{2,1,0:T(8,128)(2,1)}, u32[]{:S(2)}) copy-start(bf16[1,128,512]{2,1,0:T(8,128)(2,1)} %param.16) | copy-start | bytes 393220
  36.6 57.7 %all-to-all-start.1 = ((bf16[256,16,2,128]{3,1,2,0:T(8,128)(2,1)}), bf16[256,16,2,128]{3,1,2,0:T(8,128)(2,1)S(1)}, u32[]{:S(2)}, u32[]{:S(2)}) async-start(bf16[256,16,2,128]{3,1,2,0:T(8,128)(2,1)} %bitcast.6), calls=%async_computation.1 | async-start | bytes 4194304 | tf_op jit(solution)/shard_map/all_to_all | solution.py:76
  41.3 123.4 %all-gather.5.cloned.1.call-start = ((), (), s32[]{:S(2)}) async-start(), calls=%async_computation.4 | async-start | bytes 2228224 | tf_op jit(solution)/shard_map/all_gather | solution.py:91
  41.3 50.9 %collective-permute-start.1 = (bf16[128,512]{1,0:T(8,128)(2,1)S(1)}, bf16[128,512]{1,0:T(8,128)(2,1)S(1)}, u32[]{:S(2)}, u32[]{:S(2)}) collective-permute-start(bf16[128,512]{1,0:T(8,128)(2,1)S(1)} %bitcast.43), channel_id=1, source_target_pairs={{0,128},{128,256},{256,384},{384,0},{1,129},{129,257},{257,385},{3... | collective-permute-start | bytes 393224 | tf_op jit(solution)/shard_map/ppermute | solution.py:90
  92.3 0.7 copy-start.10
  97.7 3.3 %copy-start = (f32[2,256,128]{2,1,0:T(8,128)S(1)}, f32[2,256,128]{2,1,0:T(8,128)}, u32[]{:S(2)}) copy-start(f32[2,256,128]{2,1,0:T(8,128)} %constant.14.clone.twist) | copy-start | bytes 786436
  97.7 3.3 %copy-start.1 = (bf16[512,128]{1,0:T(8,128)(2,1)S(1)}, bf16[512,128]{1,0:T(8,128)(2,1)}, u32[]{:S(2)}) copy-start(bf16[512,128]{1,0:T(8,128)(2,1)} %constant.21.m1) | copy-start | bytes 393220
  97.7 3.3 %copy-start.2 = (bf16[256,256]{1,0:T(8,128)(2,1)S(1)}, bf16[256,256]{1,0:T(8,128)(2,1)}, u32[]{:S(2)}) copy-start(bf16[256,256]{1,0:T(8,128)(2,1)} %constant.22.m2) | copy-start | bytes 393220
  97.7 3.3 %copy-start.3 = (bf16[256,256]{1,0:T(8,128)(2,1)S(1)}, bf16[256,256]{1,0:T(8,128)(2,1)}, u32[]{:S(2)}) copy-start(bf16[256,256]{1,0:T(8,128)(2,1)} %constant.23.m3) | copy-start | bytes 393220
  97.7 3.3 %copy-start.4 = (bf16[128,512]{1,0:T(8,128)(2,1)S(1)}, bf16[128,512]{1,0:T(8,128)(2,1)}, u32[]{:S(2)}) copy-start(bf16[128,512]{1,0:T(8,128)(2,1)} %constant.24.m4) | copy-start | bytes 393220
  109.4 7.4 %copy-start.11 = (bf16[1,256]{1,0:T(2,128)(2,1)S(1)}, bf16[1,256]{1,0:T(2,128)(2,1)}, u32[]{:S(2)}) copy-start(bf16[1,256]{1,0:T(2,128)(2,1)} %param.15) | copy-start | bytes 1540
  110.6 24.4 %all-to-all-start.2 = ((bf16[16,128,128]{2,0,1:T(8,128)(2,1)}), bf16[16,128,128]{2,0,1:T(8,128)(2,1)S(1)}, u32[]{:S(2)}, u32[]{:S(2)}) async-start(bf16[16,128,128]{2,0,1:T(8,128)(2,1)} %copy.29), calls=%async_computation.2 | async-start | bytes 1048576 | tf_op jit(solution)/shard_map/all_to_all | solution.py:81
  116.7 113.1 %all-gather.3.cloned.1.call-start = ((), (), s32[]{:S(2)}) async-start(), calls=%async_computation.3 | async-start | bytes 4718592 | tf_op jit(solution)/shard_map/all_gather | solution.py:92
  135.1 1.0 copy-start.6
  135.1 1.2 copy-start.8
  136.5 16.8 %collective-permute-start = (bf16[1024,256]{1,0:T(8,128)(2,1)S(1)}, bf16[1024,256]{1,0:T(8,128)(2,1)S(1)}, u32[]{:S(2)}, u32[]{:S(2)}) collective-permute-start(bf16[1024,256]{1,0:T(8,128)(2,1)S(1)} %fusion.1), channel_id=1, source_target_pairs={{0,128},{128,256},{256,384},{384,0},{1,129},{129,257},{257,385},{3... | collective-permute-start | bytes 1572872 | tf_op jit(solution)/shard_map/ppermute | solution.py:89
  153.3 0.8 copy-start.9
Sparse Core Ops, SparseCore 0:
  93.1 71.5 all-gather.4
  166.7 63.0 all-gather.2

commit v2 on v1

v2 whole, which is shorter than its diff:
```python
import functools
import math

import jax
import jax.numpy as jnp
import numpy as np
from jax import lax
from jax.experimental import pallas as pl
from jax.experimental.pallas import tpu as pltpu
from jax.sharding import PartitionSpec as P

CHUNKS = 2
MESH = pl.DeviceIdType.MESH


def tables(rows, cols, count):
    total = rows * cols
    half = rows // 2
    k1 = np.arange(rows)
    angle = 2.0 * math.pi / rows * ((k1[:, None] * np.arange(half)[None, :]) % rows)
    single = np.concatenate([np.cos(angle), -np.sin(angle)], axis=0)
    first = np.zeros((2, 2 * rows, count, 2, half // count))
    for c in range(2):
        first[c, :, :, c, :] = single.reshape(2 * rows, count, half // count)
    first = first.reshape(4 * rows, 2 * half)
    s = np.arange(cols)
    angle = 2.0 * math.pi / cols * ((s[:, None] * s[None, :]) % cols)
    c, d = np.cos(angle), np.sin(angle)
    second = np.block([[c, -d], [d, c]])
    third = np.block([[c, d], [-d, c]])
    angle = 2.0 * math.pi / rows * ((np.arange(half)[:, None] * k1[None, :]) % rows)
    fourth = np.concatenate([np.cos(angle), -np.sin(angle)], axis=1) / total
    angle = 2.0 * math.pi / total * ((k1[:, None] * s[None, :]) % total)
    twist = np.stack([np.cos(angle), np.sin(angle)])
    cast = lambda m: jnp.asarray(m.astype(np.float32)).astype(jnp.bfloat16)
    eye = cast(np.eye(cols))
    return cast(first), cast(second), cast(third), cast(fourth), jnp.asarray(twist.astype(np.float32)), eye


def dot(a, b):
    return jnp.dot(a, b, preferred_element_type=jnp.float32)


def kernel(
    n, nz, ns, sp, sf, gate, skip, w_ref, m1, m2, m3, m4, twist, eye, out,
    rp, rf, xs, so, ro, of, feat, wf, acc, gr,
    loc, p_sem, g_sem, f_sem, o_sem, wy_sem, wx_sem, ring_s, ring_r,
):
    me, z, sec = lax.axis_index("ctx"), lax.axis_index("tensor"), lax.axis_index("section")
    ny = math.isqrt(n)
    mx, my = me // ny, me % ny
    after, before = lax.rem(sec + 1, ns), lax.rem(sec + ns - 1, ns)
    zr, zl = lax.rem(z + 1, nz), lax.rem(z + nz - 1, nz)
    rows, cols = twist.shape[1:]
    pairs = rp.shape[1]
    own = pl.ds(pl.multiple_of(16 * me, 16), 16)

    barrier = pltpu.get_barrier_semaphore()

    @pl.loop(1, n)
    def _(i):
        pl.semaphore_signal(barrier, inc=1, device_id={"ctx": lax.rem(me + i, n)}, device_id_type=MESH)

    @pl.loop(0, n)
    def _(i):
        pl.semaphore_signal(
            barrier, inc=1, device_id={"section": before, "ctx": lax.rem(me + i, n)}, device_id_type=MESH
        )

    for zz in (zr, zl):
        pl.semaphore_signal(barrier, inc=1, device_id={"tensor": zz}, device_id_type=MESH)
    pl.semaphore_wait(barrier, 2 * n + 1)

    def remote(src, dst, send, recv, where):
        return pltpu.make_async_remote_copy(
            src_ref=src, dst_ref=dst, send_sem=send, recv_sem=recv, device_id=where, device_id_type=MESH
        )

    def send_p(i):
        d = lax.rem(me + i, n)
        return remote(sp.at[:, d], rp.at[:, :, own], p_sem.at[0], p_sem.at[1], {"ctx": d})

    def send_f(g, i):
        d = lax.rem(me + i, n)
        return remote(sf.at[g, d], rf.at[g, :, own], f_sem.at[g, 0], f_sem.at[g, 1], {"ctx": d})

    def send_o(g, i):
        d = lax.rem(me + i, n)
        return remote(so.at[g, d], ro.at[g, me], o_sem.at[g, 0], o_sem.at[g, 1], {"section": after, "ctx": d})

    def send_wy(i):
        d = mx * ny + lax.rem(my + i, ny)
        return remote(w_ref, wf.at[me], wy_sem.at[0], wy_sem.at[1], {"section": after, "ctx": d})

    mine_w = wf.at[pl.ds(mx * ny, ny)]

    def send_wx(i):
        d = lax.rem(mx + i, n // ny) * ny + my
        return remote(mine_w, mine_w, wx_sem.at[0], wx_sem.at[1], {"ctx": d})

    def wait_bytes(ref, sem):
        pltpu.make_async_copy(ref, ref, sem).wait()

    local = [pltpu.make_async_copy(sp.at[:, me], rp.at[:, :, own], loc.at[0])]
    for g in range(CHUNKS):
        local.append(pltpu.make_async_copy(sf.at[g, me], rf.at[g, :, own], loc.at[1 + g]))

    @pl.loop(1, n)
    def _(i):
        send_p(i).start()

    @pl.loop(1, n)
    def _(i):
        send_f(0, i).start()

    for copy in local:
        copy.start()

    @pl.loop(0, ny)
    def _(i):
        send_wy(i).start()

    send_gate = remote(gate, gr, g_sem.at[0], g_sem.at[1], {"section": after})
    send_gate.start()

    @pl.loop(1, n)
    def _(i):
        send_f(1, i).start()

    for copy in local:
        copy.wait()
    wait_bytes(rp.at[:, :, pl.ds(0, 16 * (n - 1))], p_sem.at[1])

    for g in range(CHUNKS):
        @pl.loop(0, pairs)
        def _(p, g=g):
            y = dot(m1[...], rp[g, p])
            for c in range(2):
                yr = y[2 * c * rows : (2 * c + 1) * rows]
                yi = y[(2 * c + 1) * rows : (2 * c + 2) * rows]
                t = jnp.concatenate([yr * twist[0] + yi * twist[1], yi * twist[0] - yr * twist[1]], axis=1)
                xs[g, 2 * p + c] = dot(t.astype(jnp.bfloat16), m2[...])

    wait_bytes(mine_w, wy_sem.at[1])

    @pl.loop(1, n // ny)
    def _(i):
        send_wx(i).start()

    def inverse(g):
        wait_bytes(rf.at[g, :, pl.ds(0, 16 * (n - 1))], f_sem.at[g, 1])

        @pl.loop(0, pairs)
        def _(p):
            made = []
            px = rp[g, p].astype(jnp.float32).reshape(n, 2, 8, cols)
            for c in range(2):
                x = xs[g, 2 * p + c]
                xr, xi = x[:, :cols], x[:, cols:]
                hr = rf[g, 2 * p + c, :, :cols].astype(jnp.float32)
                hi = rf[g, 2 * p + c, :, cols:].astype(jnp.float32)
                q = jnp.concatenate([xr * hr - xi * hi, xr * hi + xi * hr], axis=1)
                v = dot(q.astype(jnp.bfloat16), m3[...])
                vr, vi = v[:, :cols], v[:, cols:]
                v = jnp.concatenate([vr * twist[0] - vi * twist[1], vi * twist[0] + vr * twist[1]], axis=0)
                o = dot(m4[...], v.astype(jnp.bfloat16)).reshape(n, 1, 8, cols)
                made.append(o + px[:, c : c + 1] * skip[g, 2 * p + c].reshape(1, 1, 1, cols))
            both = jnp.concatenate(made, axis=1).reshape(n, 16, cols)
            so[g, :, p] = both.astype(jnp.bfloat16)

        @pl.loop(0, n)
        def _(i):
            send_o(g, i).start()

    def gating(g):
        wait_bytes(ro.at[g], o_sem.at[g, 1])
        of[...] = ro[g].reshape(of.shape).astype(jnp.float32)
        for r in range(8):
            block = of[pl.ds(r, cols, stride=8), :].astype(jnp.bfloat16)
            turned = lax.dot_general(eye[...], block, (((1,), (1,)), ((), ())), preferred_element_type=jnp.float32)
            tok = pl.ds(r * cols, cols)
            h = turned * gr[tok, g * cols : (g + 1) * cols].astype(jnp.float32)
            feat[g, z, tok, :] = h.astype(jnp.bfloat16)

    toks = feat.shape[2]
    far = nz // 2

    def ring(g, k, way):
        origin = lax.rem(z - k + nz, nz) if way == 0 else lax.rem(z + k, nz)
        ref = feat.at[g, origin]
        if k == far - 1:
            ref = ref.at[pl.ds(way * (toks // 2), toks // 2)]
        return remote(ref, ref, ring_s.at[g, way, k], ring_r.at[g, way, k], {"tensor": zr if way == 0 else zl})

    def ring_step(g, k):
        for way in range(2):
            if k > 0:
                ring(g, k - 1, way).wait_recv()
            if k < far:
                ring(g, k, way).start()

    def block_of(g, offsets, tok):
        where = [lax.rem(z + k + nz, nz) for k in offsets]
        left = jnp.concatenate([feat[g, o, tok, :] for o in where], axis=1)
        right = jnp.concatenate([wf[CHUNKS * o + g] for o in where], axis=0)
        return dot(left, right)

    tile = min(256, toks)

    def project(g, offsets, how):
        @pl.loop(0, toks // tile)
        def _(t):
            tok = pl.ds(pl.multiple_of(t * tile, tile), tile)
            value = block_of(g, offsets, tok)
            if how == "set":
                acc[tok, :] = value
            elif how == "add":
                acc[tok, :] += value
            else:
                out[tok, :] = (acc[tok, :] + value).astype(out.dtype)

    inverse(0)
    send_gate.wait_recv()
    gating(0)
    for k in range(far - 1):
        ring_step(0, k)
    inverse(1)
    for k in range(far - 1, far + 1):
        ring_step(0, k)
    gating(1)
    ring_step(1, 0)
    far_w = wf.at[pl.ds(0, n - ny)]
    wait_bytes(far_w, wx_sem.at[1])
    project(0, list(range(nz)), "set")
    for k in range(1, far):
        ring_step(1, k)
        project(1, [0] if k == 1 else [1 - k, k - 1], "add")
    ring_step(1, far)
    project(1, [1 - far, far - 1, far], "out")

    send_gate.wait_send()
    wait_bytes(sp.at[:, pl.ds(0, n - 1)], p_sem.at[0])
    for g in range(CHUNKS):
        wait_bytes(sf.at[g, pl.ds(0, n - 1)], f_sem.at[g, 0])
        wait_bytes(so.at[g], o_sem.at[g, 0])
        for way in range(2):
            for k in range(far):
                ring(g, k, way).wait_send()
    wait_bytes(mine_w, wy_sem.at[0])
    wait_bytes(far_w, wx_sem.at[0])


def per_device(gate_in, value_in, gate_out, filter_spectrum, skip, out_weight):
    n, nz, ns = lax.axis_size("ctx"), lax.axis_size("tensor"), lax.axis_size("section")
    products = (gate_in[0].astype(jnp.float32) * value_in[0].astype(jnp.float32)).astype(jnp.bfloat16)
    toks, chans = products.shape
    k1s, _, cols, _ = filter_spectrum.shape[1:]
    feats = out_weight.shape[2]
    rows = n * k1s
    each = chans // (n * CHUNKS)
    pairs = each // 2
    sf = filter_spectrum[0].transpose(3, 0, 1, 2).reshape(CHUNKS, n, each, k1s, 2 * cols)
    sp = products.reshape(toks // cols, cols, chans).transpose(2, 0, 1).reshape(CHUNKS, n, pairs, 16, cols)
    mine = skip[0].astype(jnp.float32).reshape(CHUNKS, n, each)
    mine = lax.dynamic_index_in_dim(mine, lax.axis_index("ctx"), axis=1, keepdims=False)
    mine = jnp.broadcast_to(mine[:, :, None, None], (CHUNKS, each, 1, cols))
    consts = tables(rows, cols, n)
    vmem = pl.BlockSpec(memory_space=pltpu.VMEM)
    bf, f32 = jnp.bfloat16, jnp.float32
    dma = pltpu.SemaphoreType.DMA
    out = pl.pallas_call(
        functools.partial(kernel, n, nz, ns),
        out_shape=jax.ShapeDtypeStruct((toks, feats), bf),
        in_specs=[vmem] * (5 + len(consts)),
        out_specs=vmem,
        scratch_shapes=[
            pltpu.VMEM((CHUNKS, pairs, 16 * n, cols), bf),
            pltpu.VMEM((CHUNKS, each, rows, 2 * cols), bf),
            pltpu.VMEM((CHUNKS, each, rows, 2 * cols), f32),
            pltpu.VMEM((CHUNKS, n, pairs, 16, cols), bf),
            pltpu.VMEM((CHUNKS, n, pairs, 16, cols), bf),
            pltpu.VMEM((n * pairs * 16, cols), f32),
            pltpu.VMEM((CHUNKS, nz, toks, chans // CHUNKS), bf),
            pltpu.VMEM((n, *out_weight.shape[1:]), bf),
            pltpu.VMEM((toks, feats), f32),
            pltpu.VMEM((toks, chans), bf),
            dma((1 + CHUNKS,)),
            dma((2,)),
            dma((2,)),
            dma((CHUNKS, 2)),
            dma((CHUNKS, 2)),
            dma((2,)),
            dma((2,)),
            dma((CHUNKS, 2, nz // 2)),
            dma((CHUNKS, 2, nz // 2)),
        ],
        cost_estimate=pl.CostEstimate(flops=6_000_000_000, bytes_accessed=8_000_000, transcendentals=0),
        compiler_params=pltpu.CompilerParams(
            collective_id=0, has_side_effects=True, vmem_limit_bytes=56 * 1024 * 1024
        ),
    )(sp, sf, gate_out[0], mine, out_weight[0], *consts)
    return out[None]


def solution(mesh):
    placed = (
        P("section", "ctx", "tensor"),
        P("section", "ctx", "tensor"),
        P("section", "ctx", "tensor"),
        P("section", "ctx", None, None, "tensor"),
        P("section", "tensor"),
        P("section", "ctx", "tensor"),
    )
    return jax.shard_map(
        per_device,
        mesh=mesh,
        in_specs=placed,
        out_specs=P("section", "ctx", "tensor"),
        check_vma=False,
    )
```

time: 246 us -> 170 us (0.69)
  the two profiles are of different devices: /device:TPU:1 before, /device:TPU:8 now
where the time goes in v2:
time: 170 us; the launch traced here: 169 us
  Pallas kernels  157 us (92%)
  local copies, waits for them, and re-layouts  11.7 us (7%)
    pallas_call x1, Pallas kernels, per_device(): pl.pallas_call(functools.partial(kernel, n, nz, ns), out_shape=jax.ShapeD...  157 us
    transpose x1, local copies, waits for them, and re-layouts, per_device(): filter_spectrum[0].transpose(3, 0, 1, 2)  4.94 us

profile of v2, /device:TPU:8, one launch (start us, length us, event | category | flops | bytes accessed | tf_op | source)
XLA Modules:
  0.0 169.3 jit_solution(10930752649462102067)
XLA Ops:
  0.0 0.7 convert_reduce_fusion
  0.7 0.1 reshape.23
  0.8 0.7 broadcast_in_dim.12.skip
  1.5 4.9 %copy.17 = bf16[256,16,2,128]{3,2,1,0:T(2,128)(2,1)S(1)} copy(bf16[256,16,2,128]{0,3,2,1:T(8,128)(2,1)} %bitcast.12) | data formatting | bytes 4194304 | tf_op jit(solution)/shard_map/transpose | solution.py:262
  6.4 0.0 copy-start
  6.4 0.0 copy-start.1
  6.4 2.6 %reshape.22.sf = bf16[2,16,8,16,256]{4,3,2,1,0:T(8,128)(2,1)} reshape(bf16[256,16,2,128]{3,2,1,0:T(2,128)(2,1)S(1)} %copy.17) | data formatting | bytes 4194304 | tf_op jit(solution)/shard_map/reshape | solution.py:262
  9.1 0.0 copy-done
  9.1 0.0 copy-done.1
  9.1 0.1 multiply_convert_fusion
  9.2 1.1 copy.16
  10.3 156.7 %shard_map.118 = bf16[1024,512]{1,0:T(8,128)(2,1)} custom-call(bf16[2,16,4,16,128]{4,3,2,1,0:T(8,128)(2,1)} %bitcast.14, bf16[2,16,8,16,256]{4,3,2,1,0:T(8,128)(2,1)} %reshape.22.sf, bf16[1024,256]{1,0:T(8,128)(2,1)} %bitcast.16, f32[2,8,1,128]{3,2,1,0:T(1,128)} %broadcast_in_dim.12.skip, bf16[128,512]{1,0:T(8,128)(2,1)} %bitcast.17, ...), custom_call_target="tpu_custom_call" | custom-call | flops 6000000000 | bytes 8000000 | tf_op jit(solution)/shard_map/pallas_call | solution.py:271
  167.0 2.3 %copy.19 = bf16[1,1024,512]{2,1,0:T(8,128)(2,1)} copy(bf16[1,1024,512]{2,1,0:T(8,128)(2,1)} %bitcast.13) | data formatting | bytes 2097152
  (1 shorter events, 0.0 us)
Async XLA Ops:
  6.4 2.7 %copy-start = (bf16[1,1024,256]{2,1,0:T(8,128)(2,1)S(1)}, bf16[1,1024,256]{2,1,0:T(8,128)(2,1)}, u32[]{:S(2)}) copy-start(bf16[1,1024,256]{2,1,0:T(8,128)(2,1)} %param.13) | copy-start | bytes 1572868
  6.4 2.7 %copy-start.1 = (bf16[1,1024,256]{2,1,0:T(8,128)(2,1)S(1)}, bf16[1,1024,256]{2,1,0:T(8,128)(2,1)}, u32[]{:S(2)}) copy-start(bf16[1,1024,256]{2,1,0:T(8,128)(2,1)} %param.12) | copy-start | bytes 1572868

commit v3 on v2

v3 whole, which is shorter than its diff:
```python
import functools
import math

import jax
import jax.numpy as jnp
import numpy as np
from jax import lax
from jax.experimental import pallas as pl
from jax.experimental.pallas import tpu as pltpu
from jax.sharding import PartitionSpec as P

CHUNKS = 4
PIECES = 4
MESH = pl.DeviceIdType.MESH


def tables(rows, cols, count):
    total = rows * cols
    half = rows // 2
    k1 = np.arange(rows)
    angle = 2.0 * math.pi / rows * ((k1[:, None] * np.arange(half)[None, :]) % rows)
    single = np.concatenate([np.cos(angle), -np.sin(angle)], axis=0)
    first = np.zeros((2, 2 * rows, count, 2, half // count))
    for c in range(2):
        first[c, :, :, c, :] = single.reshape(2 * rows, count, half // count)
    first = first.reshape(4 * rows, 2 * half)
    s = np.arange(cols)
    angle = 2.0 * math.pi / cols * ((s[:, None] * s[None, :]) % cols)
    c, d = np.cos(angle), np.sin(angle)
    second = np.block([[c, -d], [d, c]])
    third = np.block([[c, d], [-d, c]])
    angle = 2.0 * math.pi / rows * ((np.arange(half)[:, None] * k1[None, :]) % rows)
    fourth = np.concatenate([np.cos(angle), -np.sin(angle)], axis=1) / total
    angle = 2.0 * math.pi / total * ((k1[:, None] * s[None, :]) % total)
    twist = np.stack([np.cos(angle), np.sin(angle)])
    cast = lambda m: jnp.asarray(m.astype(np.float32)).astype(jnp.bfloat16)
    eye = cast(np.eye(cols))
    return cast(first), cast(second), cast(third), cast(fourth), jnp.asarray(twist.astype(np.float32)), eye


def dot(a, b):
    return jnp.dot(a, b, preferred_element_type=jnp.float32)


def turn(eye, block):
    return lax.dot_general(eye, block, (((1,), (1,)), ((), ())), preferred_element_type=jnp.float32)


def kernel(
    n, nz, ns, gate_in, value_in, f_ref, gate, skip, w_ref, m1, m2, m3, m4, twist, eye, out,
    f_in, wide, sp, sf, rp, rf, xs, so, ro, feat, wf, acc, gr,
    loc, p_sem, g_sem, f_sem, o_sem, wy_sem, wx_sem, ring_s, ring_r,
):
    me, z, sec = lax.axis_index("ctx"), lax.axis_index("tensor"), lax.axis_index("section")
    ny = math.isqrt(n)
    mx, my = me // ny, me % ny
    after, before = lax.rem(sec + 1, ns), lax.rem(sec + ns - 1, ns)
    zr, zl = lax.rem(z + 1, nz), lax.rem(z + nz - 1, nz)
    rows, cols = twist.shape[1:]
    pairs = rp.shape[1]
    each = 2 * pairs
    chans = gate_in.shape[1]
    width = chans // CHUNKS
    own = pl.ds(pl.multiple_of(16 * me, 16), 16)

    load_f = pltpu.make_async_copy(f_ref, f_in, loc.at[0])
    load_f.start()
    barrier = pltpu.get_barrier_semaphore()

    @pl.loop(1, n)
    def _(i):
        pl.semaphore_signal(barrier, inc=1, device_id={"ctx": lax.rem(me + i, n)}, device_id_type=MESH)

    @pl.loop(0, n)
    def _(i):
        pl.semaphore_signal(
            barrier, inc=1, device_id={"section": before, "ctx": lax.rem(me + i, n)}, device_id_type=MESH
        )

    for zz in (zr, zl):
        pl.semaphore_signal(barrier, inc=1, device_id={"tensor": zz}, device_id_type=MESH)

    for r in range(8):
        tok = slice(r * cols, (r + 1) * cols)
        for h in range(chans // cols):
            lanes = slice(h * cols, (h + 1) * cols)
            prod = gate_in[tok, lanes].astype(jnp.float32) * value_in[tok, lanes].astype(jnp.float32)
            wide[0, pl.ds(h * cols * 8 + r, cols, stride=8), :] = turn(eye[...], prod.astype(jnp.bfloat16))
    part = 8 * chans // CHUNKS
    for g in range(CHUNKS):
        block = wide[0, g * part : (g + 1) * part, :].astype(jnp.bfloat16)
        sp[g] = block.reshape(n, pairs, 16, cols)

    pl.semaphore_wait(barrier, 2 * n + 1)

    def remote(src, dst, send, recv, where):
        return pltpu.make_async_remote_copy(
            src_ref=src, dst_ref=dst, send_sem=send, recv_sem=recv, device_id=where, device_id_type=MESH
        )

    def send_p(i):
        d = lax.rem(me + i, n)
        return remote(sp.at[:, d], rp.at[:, :, own], p_sem.at[0], p_sem.at[1], {"ctx": d})

    def send_f(g, i):
        d = lax.rem(me + i, n)
        return remote(sf.at[g, d], rf.at[g, :, own], f_sem.at[g, 0], f_sem.at[g, 1], {"ctx": d})

    def send_o(g, i):
        d = lax.rem(me + i, n)
        return remote(so.at[g, d], ro.at[g, me], o_sem.at[g, 0], o_sem.at[g, 1], {"section": after, "ctx": d})

    def send_wy(i):
        d = mx * ny + lax.rem(my + i, ny)
        return remote(w_ref, wf.at[me], wy_sem.at[0], wy_sem.at[1], {"section": after, "ctx": d})

    mine_w = wf.at[pl.ds(mx * ny, ny)]
    far_w = wf.at[pl.ds(0, n - ny)]

    def send_wx(i):
        d = lax.rem(mx + i, n // ny) * ny + my
        return remote(mine_w, mine_w, wx_sem.at[0], wx_sem.at[1], {"ctx": d})

    def wait_bytes(ref, sem):
        pltpu.make_async_copy(ref, ref, sem).wait()

    def start_all(copy, first, last):
        @pl.loop(first, last)
        def _(i):
            copy(i).start()

    own_p = pltpu.make_async_copy(sp.at[:, me], rp.at[:, :, own], loc.at[1])

    def own_f(g):
        return pltpu.make_async_copy(sf.at[g, me], rf.at[g, :, own], loc.at[2 + g])

    start_all(send_p, 1, n)
    own_p.start()

    def turn_spectrum(h):
        for k in range(16):
            block = f_in[k, :, :, h * cols : (h + 1) * cols].reshape(2 * cols, cols)
            turned = turn(eye[...], block)
            for c in range(2):
                wide[c, pl.ds(k, cols, stride=16), :] = turned[:, c * cols : (c + 1) * cols]
        for g in range(2):
            size = 8 * cols
            block = jnp.concatenate([wide[c, g * size : (g + 1) * size, :] for c in range(2)], axis=1).astype(jnp.bfloat16)
            sf[2 * h + g] = block.reshape(n, each, 16, 2 * cols)
            own_f(2 * h + g).start()

    def start_f(g):
        start_all(functools.partial(send_f, g), 1, n)

    def sent_f(g):
        wait_bytes(sf.at[g, pl.ds(0, n - 1)], f_sem.at[g, 0])

    load_f.wait()
    turn_spectrum(0)
    start_f(0)
    send_gate = remote(gate, gr, g_sem.at[0], g_sem.at[1], {"section": after})
    send_gate.start()
    start_all(send_wy, 0, ny)
    turn_spectrum(1)

    own_p.wait()
    wait_bytes(rp.at[:, :, pl.ds(0, 16 * (n - 1))], p_sem.at[1])

    for g in range(CHUNKS):
        @pl.loop(0, pairs)
        def _(p, g=g):
            y = dot(m1[...], rp[g, p])
            for c in range(2):
                yr = y[2 * c * rows : (2 * c + 1) * rows]
                yi = y[(2 * c + 1) * rows : (2 * c + 2) * rows]
                t = jnp.concatenate([yr * twist[0] + yi * twist[1], yi * twist[0] - yr * twist[1]], axis=1)
                xs[g, 2 * p + c] = dot(t.astype(jnp.bfloat16), m2[...])

    def inverse(g):
        own_f(g).wait()
        wait_bytes(rf.at[g, :, pl.ds(0, 16 * (n - 1))], f_sem.at[g, 1])

        @pl.loop(0, pairs)
        def _(p):
            made = []
            px = rp[g, p].astype(jnp.float32).reshape(n, 2, 8, cols)
            for c in range(2):
                x = xs[g, 2 * p + c]
                xr, xi = x[:, :cols], x[:, cols:]
                hr = rf[g, 2 * p + c, :, :cols].astype(jnp.float32)
                hi = rf[g, 2 * p + c, :, cols:].astype(jnp.float32)
                q = jnp.concatenate([xr * hr - xi * hi, xr * hi + xi * hr], axis=1)
                v = dot(q.astype(jnp.bfloat16), m3[...])
                vr, vi = v[:, :cols], v[:, cols:]
                v = jnp.concatenate([vr * twist[0] - vi * twist[1], vi * twist[0] + vr * twist[1]], axis=0)
                o = dot(m4[...], v.astype(jnp.bfloat16)).reshape(n, 1, 8, cols)
                made.append(o + px[:, c : c + 1] * skip[0, g * width + each * me + 2 * p + c])
            both = jnp.concatenate(made, axis=1).reshape(n, 16, cols)
            so[g, :, p] = both.astype(jnp.bfloat16)

        start_all(functools.partial(send_o, g), 0, n)

    lane = lax.broadcasted_iota(jnp.int32, (cols, cols), 1)

    def gating(g):
        wait_bytes(ro.at[g], o_sem.at[g, 1])
        wide[0, 0 : 8 * width, :] = ro[g].reshape(8 * width, cols).astype(jnp.float32)
        lanes = slice(g // 2 * cols, (g // 2 + 1) * cols)
        for r in range(4):
            picked = [wide[0, pl.ds(k, width, stride=8), :] for k in (r, r + 4)]
            low = gr[r * cols : (r + 1) * cols, lanes].astype(jnp.float32)
            high = gr[(r + 4) * cols : (r + 5) * cols, lanes].astype(jnp.float32)
            high = pltpu.roll(high, width, 1)
            if g % 2 == 1:
                picked = picked[::-1]
                by = jnp.where(lane < width, high, low)
            else:
                by = jnp.where(lane < width, low, high)
            turned = turn(eye[...], jnp.concatenate(picked, axis=0).astype(jnp.bfloat16))
            feat[g, z, r * cols : (r + 1) * cols, :] = (turned * by).astype(jnp.bfloat16)

    toks = feat.shape[2]
    far = nz // 2

    def ring(g, k, way, piece):
        origin = lax.rem(z - k + nz, nz) if way == 0 else lax.rem(z + k, nz)
        size = toks // PIECES
        first = piece * size
        if k == far - 1:
            size = size // 2
            first = way * (toks // 2) + piece * size
        ref = feat.at[g, origin, pl.ds(first, size)]
        where = {"tensor": zr if way == 0 else zl}
        return remote(ref, ref, ring_s.at[g, way, k, piece], ring_r.at[g, way, k, piece], where)

    def arrived(g, k, way, piece):
        if k == far - 1:
            half = PIECES // 2
            if piece % 2 == 0:
                for p in range(half * way + piece // 2, half * way + piece // 2 + 1):
                    ring(g, k - 1, way, p).wait_recv()
        else:
            ring(g, k - 1, way, piece).wait_recv()

    def ring_step(g, k):
        for piece in range(PIECES):
            for way in range(2):
                if k > 0:
                    arrived(g, k, way, piece)
                if k < far:
                    ring(g, k, way, piece).start()
        if k == far - 1:
            for way in range(2):
                for p in range(PIECES // 2):
                    ring(g, k - 1, way, (1 - way) * (PIECES // 2) + p).wait_recv()

    tile = min(128, toks)
    tile_lane = lax.broadcasted_iota(jnp.int32, (tile, cols), 1)

    def project(h, offsets, how):
        where = [lax.rem(z + k + nz, nz) for k in offsets]

        @pl.loop(0, toks // tile)
        def _(t):
            tok = pl.ds(pl.multiple_of(t * tile, tile), tile)
            even = [feat[2 * h, o, tok, :] for o in where]
            odd = [feat[2 * h + 1, o, tok, :] for o in where]
            for half in range(2):
                first, second = (even, odd) if half == 0 else (odd, even)
                left = jnp.concatenate([jnp.where(tile_lane < width, a, b) for a, b in zip(first, second)], axis=1)
                right = []
                for o in where:
                    w = wf[2 * o + h]
                    right += [w] if half == 0 else [w[width:], w[:width]]
                value = dot(left, jnp.concatenate(right, axis=0))
                to = pl.ds(pl.multiple_of(half * toks + t * tile, tile), tile)
                if how == "set":
                    acc[to, :] = value
                elif how == "add":
                    acc[to, :] += value
                else:
                    out[to, :] = (acc[to, :] + value).astype(out.dtype)

    for g in range(CHUNKS):
        if g == 0:
            sent_f(0)
            start_f(1)
        inverse(g)
        if g == 0:
            wait_bytes(mine_w, wy_sem.at[1])
            start_all(send_wx, 1, n // ny)
            send_gate.wait_recv()
        else:
            for k in range(2, far):
                ring_step(g - 1, k)
        gating(g)
        ring_step(g, 0)
        if g + 2 < CHUNKS:
            sent_f(g + 1)
            start_f(g + 2)
        if g > 0:
            ring_step(g - 1, far)
        if g == 2:
            wait_bytes(far_w, wx_sem.at[1])
            project(0, list(range(nz)), "set")
        ring_step(g, 1)
    last = CHUNKS - 1
    project(1, [0], "add")
    for k in range(2, far):
        ring_step(last, k)
        project(1, [1 - k, k - 1], "add")
    ring_step(last, far)
    project(1, [1 - far, far - 1, far], "out")

    send_gate.wait_send()
    wait_bytes(sp.at[:, pl.ds(0, n - 1)], p_sem.at[0])
    for g in range(CHUNKS):
        if g == CHUNKS - 1:
            sent_f(g)
        wait_bytes(so.at[g], o_sem.at[g, 0])
        for way in range(2):
            for k in range(far):
                for piece in range(PIECES):
                    ring(g, k, way, piece).wait_send()
    wait_bytes(mine_w, wy_sem.at[0])
    wait_bytes(far_w, wx_sem.at[0])


def per_device(gate_in, value_in, gate_out, filter_spectrum, skip, out_weight):
    n, nz, ns = lax.axis_size("ctx"), lax.axis_size("tensor"), lax.axis_size("section")
    toks, chans = gate_in.shape[1:]
    k1s, _, cols, _ = filter_spectrum.shape[1:]
    feats = out_weight.shape[2]
    rows = n * k1s
    each = chans // (n * CHUNKS)
    pairs = each // 2
    consts = tables(rows, cols, n)
    vmem = pl.BlockSpec(memory_space=pltpu.VMEM)
    anywhere = pl.BlockSpec(memory_space=pl.ANY)
    bf, f32 = jnp.bfloat16, jnp.float32
    dma = pltpu.SemaphoreType.DMA
    out = pl.pallas_call(
        functools.partial(kernel, n, nz, ns),
        out_shape=jax.ShapeDtypeStruct((toks, feats), bf),
        in_specs=[vmem, vmem, anywhere, anywhere, pl.BlockSpec(memory_space=pltpu.SMEM), anywhere] + [vmem] * len(consts),
        out_specs=vmem,
        scratch_shapes=[
            pltpu.VMEM((k1s, 2, cols, chans), bf),
            pltpu.VMEM((2, 16 * cols, cols), f32),
            pltpu.VMEM((CHUNKS, n, pairs, 16, cols), bf),
            pltpu.VMEM((CHUNKS, n, each, 16, 2 * cols), bf),
            pltpu.VMEM((CHUNKS, pairs, 16 * n, cols), bf),
            pltpu.VMEM((CHUNKS, each, rows, 2 * cols), bf),
            pltpu.VMEM((CHUNKS, each, rows, 2 * cols), f32),
            pltpu.VMEM((CHUNKS, n, pairs, 16, cols), bf),
            pltpu.VMEM((CHUNKS, n, pairs, 16, cols), bf),
            pltpu.VMEM((CHUNKS, nz, toks // 2, cols), bf),
            pltpu.VMEM((n, *out_weight.shape[1:]), bf),
            pltpu.VMEM((toks, feats), f32),
            pltpu.VMEM((toks, chans), bf),
            dma((2 + CHUNKS,)),
            dma((2,)),
            dma((2,)),
            dma((CHUNKS, 2)),
            dma((CHUNKS, 2)),
            dma((2,)),
            dma((2,)),
            dma((CHUNKS, 2, nz // 2, PIECES)),
            dma((CHUNKS, 2, nz // 2, PIECES)),
        ],
        cost_estimate=pl.CostEstimate(flops=6_000_000_000, bytes_accessed=8_000_000, transcendentals=0),
        compiler_params=pltpu.CompilerParams(
            collective_id=0, has_side_effects=True, vmem_limit_bytes=56 * 1024 * 1024
        ),
    )(gate_in[0], value_in[0], filter_spectrum[0], gate_out[0], skip.astype(f32), out_weight[0], *consts)
    return out[None]


def solution(mesh):
    placed = (
        P("section", "ctx", "tensor"),
        P("section", "ctx", "tensor"),
        P("section", "ctx", "tensor"),
        P("section", "ctx", None, None, "tensor"),
        P("section", "tensor"),
        P("section", "ctx", "tensor"),
    )
    return jax.shard_map(
        per_device,
        mesh=mesh,
        in_specs=placed,
        out_specs=P("section", "ctx", "tensor"),
        check_vma=False,
    )
```

time: 170 us -> 145 us (0.85)
  the two profiles are of different devices: /device:TPU:8 before, /device:TPU:1 now
where the time goes in v3:
time: 145 us; the launch traced here: 144 us
  Pallas kernels  141 us (97%)
  local copies, waits for them, and re-layouts  2.26 us (2%)
    pallas_call x1, Pallas kernels, per_device(): pl.pallas_call(functools.partial(kernel, n, nz, ns), out_shape=jax.ShapeD...  141 us

profile of v3, /device:TPU:1, one launch (start us, length us, event | category | flops | bytes accessed | tf_op | source)
XLA Modules:
  0.0 144.4 jit_solution(951496027779658174)
XLA Ops:
  0.0 1.2 convert_element_type.18.skip
  1.2 140.9 %shard_map.118 = bf16[1024,512]{1,0:T(8,128)(2,1)} custom-call(bf16[1024,256]{1,0:T(8,128)(2,1)} %bitcast.8, bf16[1024,256]{1,0:T(8,128)(2,1)} %bitcast.9, bf16[16,2,128,256]{3,2,1,0:T(8,128)(2,1)} %bitcast.7, bf16[1024,256]{1,0:T(8,128)(2,1)} %bitcast.10, f32[1,256]{1,0:T(1,128)} %convert_element_type.18.skip, bf16[128,512]{1,0:T(8,128)(2,1)} %bitcast.11, ...), custom_call_target="tpu_custom_call" | custom-call | flops 6000000000 | bytes 8000000 | tf_op jit(solution)/shard_map/pallas_call | solution.py:342
  142.2 2.3 %copy.14 = bf16[1,1024,512]{2,1,0:T(8,128)(2,1)} copy(bf16[1,1024,512]{2,1,0:T(8,128)(2,1)} %bitcast.6) | data formatting | bytes 2097152

commit v4 on v3

--- a/solution.py
+++ b/solution.py
@@ -10,7 +10,7 @@
 from jax.sharding import PartitionSpec as P
 
 CHUNKS = 4
-PIECES = 4
+PIECES = 2
 MESH = pl.DeviceIdType.MESH
 
 
@@ -47,9 +47,10 @@
 
 
 def kernel(
-    n, nz, ns, gate_in, value_in, f_ref, gate, skip, w_ref, m1, m2, m3, m4, twist, eye, out,
+    n, nz, ns, gate_any, value_any, f_ref, gate, skip, w_ref, m1_any, m2_any, m3_any, m4_any, twist_any, eye_any, out,
     f_in, wide, sp, sf, rp, rf, xs, so, ro, feat, wf, acc, gr,
-    loc, p_sem, g_sem, f_sem, o_sem, wy_sem, wx_sem, ring_s, ring_r,
+    gate_in, value_in, eye, m1, m2, m3, m4, twist,
+    loc, p_sem, g_sem, f_sem, o_sem, wy_sem, wx_sem, ring_s, ring_r, in_sem,
 ):
     me, z, sec = lax.axis_index("ctx"), lax.axis_index("tensor"), lax.axis_index("section")
     ny = math.isqrt(n)
@@ -64,7 +65,14 @@
     own = pl.ds(pl.multiple_of(16 * me, 16), 16)
 
     load_f = pltpu.make_async_copy(f_ref, f_in, loc.at[0])
+    pulled = ((eye_any, eye), (gate_any, gate_in), (value_any, value_in), (m1_any, m1), (m2_any, m2), (m3_any, m3),
+              (m4_any, m4), (twist_any, twist))
+    loads = [pltpu.make_async_copy(src, dst, in_sem.at[k]) for k, (src, dst) in enumerate(pulled)]
+    for k in range(3):
+        loads[k].start()
     load_f.start()
+    for k in range(3, len(loads)):
+        loads[k].start()
     barrier = pltpu.get_barrier_semaphore()
 
     @pl.loop(1, n)
@@ -80,6 +88,8 @@
     for zz in (zr, zl):
         pl.semaphore_signal(barrier, inc=1, device_id={"tensor": zz}, device_id_type=MESH)
 
+    for k in range(3):
+        loads[k].wait()
     for r in range(8):
         tok = slice(r * cols, (r + 1) * cols)
         for h in range(chans // cols):
@@ -163,6 +173,8 @@
     start_all(send_wy, 0, ny)
     turn_spectrum(1)
 
+    for k in range(3, len(loads)):
+        loads[k].wait()
     own_p.wait()
     wait_bytes(rp.at[:, :, pl.ds(0, 16 * (n - 1))], p_sem.at[1])
 
@@ -281,41 +293,45 @@
                 else:
                     out[to, :] = (acc[to, :] + value).astype(out.dtype)
 
+    sent_f(0)
+    start_f(1)
+    last = CHUNKS - 1
     for g in range(CHUNKS):
-        if g == 0:
-            sent_f(0)
-            start_f(1)
         inverse(g)
         if g == 0:
             wait_bytes(mine_w, wy_sem.at[1])
             start_all(send_wx, 1, n // ny)
             send_gate.wait_recv()
         else:
-            for k in range(2, far):
+            for k in range(2, far - 1):
                 ring_step(g - 1, k)
         gating(g)
         ring_step(g, 0)
         if g + 2 < CHUNKS:
-            sent_f(g + 1)
             start_f(g + 2)
         if g > 0:
-            ring_step(g - 1, far)
-        if g == 2:
-            wait_bytes(far_w, wx_sem.at[1])
-            project(0, list(range(nz)), "set")
-        ring_step(g, 1)
-    last = CHUNKS - 1
-    project(1, [0], "add")
+            ring_step(g - 1, far - 1)
+        if far > 2 or g == last:
+            ring_step(g, 1)
+        if g > 1:
+            ring_step(g - 2, far)
+    wait_bytes(far_w, wx_sem.at[1])
+    project(0, list(range(nz)), "set")
     for k in range(2, far):
         ring_step(last, k)
+        if k == 2:
+            ring_step(last - 1, far)
+            project(1, [0], "add")
         project(1, [1 - k, k - 1], "add")
+    if far == 2:
+        ring_step(last - 1, far)
     ring_step(last, far)
-    project(1, [1 - far, far - 1, far], "out")
+    project(1, [1 - far, far - 1, far] if far > 2 else [0, 1, -1, 2], "out")
 
     send_gate.wait_send()
     wait_bytes(sp.at[:, pl.ds(0, n - 1)], p_sem.at[0])
     for g in range(CHUNKS):
-        if g == CHUNKS - 1:
+        if g > 0:
             sent_f(g)
         wait_bytes(so.at[g], o_sem.at[g, 0])
         for way in range(2):
@@ -342,7 +358,7 @@
     out = pl.pallas_call(
         functools.partial(kernel, n, nz, ns),
         out_shape=jax.ShapeDtypeStruct((toks, feats), bf),
-        in_specs=[vmem, vmem, anywhere, anywhere, pl.BlockSpec(memory_space=pltpu.SMEM), anywhere] + [vmem] * len(consts),
+        in_specs=[anywhere] * 4 + [pl.BlockSpec(memory_space=pltpu.SMEM)] + [anywhere] * (1 + len(consts)),
         out_specs=vmem,
         scratch_shapes=[
             pltpu.VMEM((k1s, 2, cols, chans), bf),
@@ -358,6 +374,9 @@
             pltpu.VMEM((n, *out_weight.shape[1:]), bf),
             pltpu.VMEM((toks, feats), f32),
             pltpu.VMEM((toks, chans), bf),
+            pltpu.VMEM((toks, chans), bf),
+            pltpu.VMEM((toks, chans), bf),
+            *[pltpu.VMEM(c.shape, c.dtype) for c in (consts[-1], *consts[:-1])],
             dma((2 + CHUNKS,)),
             dma((2,)),
             dma((2,)),
@@ -367,6 +386,7 @@
             dma((2,)),
             dma((CHUNKS, 2, nz // 2, PIECES)),
             dma((CHUNKS, 2, nz // 2, PIECES)),
+            dma((2 + len(consts),)),
         ],
         cost_estimate=pl.CostEstimate(flops=6_000_000_000, bytes_accessed=8_000_000, transcendentals=0),
         compiler_params=pltpu.CompilerParams(

time: 145 us -> 141 us (0.972)
  Pallas kernels: 141 us -> 137 us
    pallas_call x1, Pallas kernels: 141 us -> 137 us  [per_device(): pl.pallas_call(functools.partial(kernel, n, nz, ns), out_shape=jax.ShapeD...]
where the time goes in v4:
time: 141 us
  Pallas kernels  137 us (97%)
  local copies, waits for them, and re-layouts  2.26 us (2%)
    pallas_call x1, Pallas kernels, per_device(): pl.pallas_call(functools.partial(kernel, n, nz, ns), out_shape=jax.ShapeD...  137 us

profile of v4, /device:TPU:1, one launch (start us, length us, event | category | flops | bytes accessed | tf_op | source)
XLA Modules:
  0.0 140.6 jit_solution(2545886035699255124)
XLA Ops:
  0.0 1.2 convert_element_type.18.skip
  1.2 137.1 %shard_map.118 = bf16[1024,512]{1,0:T(8,128)(2,1)} custom-call(bf16[1024,256]{1,0:T(8,128)(2,1)} %bitcast.8, bf16[1024,256]{1,0:T(8,128)(2,1)} %bitcast.9, bf16[16,2,128,256]{3,2,1,0:T(8,128)(2,1)} %bitcast.7, bf16[1024,256]{1,0:T(8,128)(2,1)} %bitcast.10, f32[1,256]{1,0:T(1,128)} %convert_element_type.18.skip, bf16[128,512]{1,0:T(8,128)(2,1)} %bitcast.11, ...), custom_call_target="tpu_custom_call" | custom-call | flops 6000000000 | bytes 8000000 | tf_op jit(solution)/shard_map/pallas_call | solution.py:358
  138.3 2.3 %copy.14 = bf16[1,1024,512]{2,1,0:T(8,128)(2,1)} copy(bf16[1,1024,512]{2,1,0:T(8,128)(2,1)} %bitcast.6) | data formatting | bytes 2097152
